TPU v7x, 32 devices: a whole 2x2x4 slice. The times are simulated.
32 devices in a mesh: outer: 2 (over y), inner: 4 (over z), head: 4 (over x, core).
Axes of the slice: x: 2, y: 2, z: 4, core: 2. Of those that a mesh axis runs over, the one named last changes fastest.
Arguments:
- queries: bfloat16 [8192, 4096], P(('outer', 'inner'), 'head'), may hold values from -6 to 6
- keys: bfloat16 [8192, 4096], P(('outer', 'inner'), 'head'), may hold values from -0.046875 to 0.046875
- values: bfloat16 [8192, 4096], P(('outer', 'inner'), 'head'), may hold values from -36 to 36
- out_grad: bfloat16 [8192, 4096], P(('outer', 'inner'), 'head'), may hold values from -6 to 6
- log_key_decay: float32 [8192, 4096], P(('outer', 'inner'), 'head'), may hold values from -0.62 to 0
- value_rate: float32 [4096], P('head'), may hold values from 1.2207031e-05 to 0.05
- norm_gain: float32 [4096], P('head'), may hold values from 0.1 to 1.9
Outputs:
- query_grad: bfloat16 [8192, 4096], P(('outer', 'inner'), 'head')
- key_grad: bfloat16 [8192, 4096], P(('outer', 'inner'), 'head')
- value_grad: bfloat16 [8192, 4096], P(('outer', 'inner'), 'head')
- gain_grad: float32 [4096], P('head')
All inputs are finite; a program needn't handle non-finite values.
Results may differ from a plain program's by a relative error of at most 0.001.
Values sent between devices are 32-bit elements; how exact they have to be, the bound alone decides.
A program may use at most 192 MiB of HBM per device.

v0:
```python
import functools
import math

import jax
import jax.numpy as jnp
from jax import lax
from jax.experimental import pallas as pl
from jax.experimental.pallas import tpu as pltpu
from jax.sharding import PartitionSpec as P

D = 128
BL = 128
MESH = pl.DeviceIdType.MESH
f32 = jnp.float32
bf16 = jnp.bfloat16


def split(x):
    high = x.astype(bf16)
    return high, (x - high.astype(f32)).astype(bf16)


def product(pairs, left_dim, right_dim):
    def dot(left, right):
        return lax.dot_general(
            left, right, (((left_dim,), (right_dim,)), ((), ())), preferred_element_type=f32
        )

    total = None
    for (ah, al), (bh, bl) in pairs:
        part = dot(ah, bh) + (dot(ah, bl) + dot(al, bh))
        total = part if total is None else total + part
    return total


def nn(*pairs):
    return product(pairs, 1, 0)


def nt(*pairs):
    return product(pairs, 1, 1)


def tn(*pairs):
    return product(pairs, 0, 0)


def kernel(
    sizes,
    q_ref, k_ref, v_ref, og_ref, decay_ref, rate_ref, gain_ref,
    qg_ref, kg_ref, vg_ref, gg_ref,
    c_ref, qh_ref, ql_ref, kh_ref, kl_ref, gh_ref, gl_ref,
    core_ref, sc_ref, start_ref, end_ref,
    last_ref, total_ref, local_ref,
    fr_ref, fs_ref, ar_ref, as_ref,
    sq_ref, cr_ref, hs_ref, gs_ref,
    fr_sem, fs_sem, ar_sem, as_sem, hr_sem, hs_sem, gr_sem, gs_sem,
):
    n_outer, n_inner, n_head = sizes
    n = n_outer * n_inner
    rows_all, cols_all = q_ref.shape
    heads = cols_all // D
    blocks = rows_all // BL
    p = lax.axis_index("outer") * n_inner + lax.axis_index("inner")
    me = lax.axis_index("head")

    def seq_device(i):
        return {"outer": i // n_inner, "inner": lax.rem(i, n_inner)}

    barrier = pltpu.get_barrier_semaphore()

    def greet_seq(i, _):
        pl.semaphore_signal(
            barrier, inc=1, device_id=seq_device(lax.rem(p + i, n)), device_id_type=MESH
        )
        return 0

    lax.fori_loop(1, n, greet_seq, 0)
    for i in range(1, n_head):
        pl.semaphore_signal(
            barrier, inc=1, device_id={"head": lax.rem(me + i, n_head)}, device_id_type=MESH
        )

    row_id = lax.broadcasted_iota(jnp.int32, (BL, BL), 0)
    col_id = lax.broadcasted_iota(jnp.int32, (BL, BL), 1)
    causal = row_id >= col_id
    steps_in = (lax.broadcasted_iota(jnp.int32, (BL, D), 0) + 1).astype(f32)
    span = float(BL)

    def rows(b):
        return pl.ds(pl.multiple_of(b * BL, BL), BL)

    def cols(h):
        return pl.ds(pl.multiple_of(h * D, D), D)

    def rate_row(h):
        return rate_ref[pl.ds(h, 1), :]

    def rate_down(h):
        return jnp.broadcast_to(rate_row(h), (D, D)).T

    def last_row(h, b):
        return last_ref[pl.ds(h * blocks + b, 1), :]

    def pieces(high, low, b, h):
        return high[rows(b), cols(h)], low[rows(b), cols(h)]

    def value_tilde(b, h, shrink):
        return split(v_ref[rows(b), cols(h)].astype(f32) * shrink)

    def prepare(h, _):
        down = rate_down(h)
        shrink = jnp.exp(steps_in * rate_row(h))
        ones = causal.astype(bf16)

        def block(b, carry):
            state, key_sum = carry
            d = decay_ref[rows(b), cols(h)]
            d1 = d.astype(bf16)
            rest = d - d1.astype(f32)
            d2 = rest.astype(bf16)
            d3 = (rest - d2.astype(f32)).astype(bf16)
            sums = jnp.dot(
                ones, jnp.concatenate([d1, d2, d3], axis=1), preferred_element_type=f32
            )
            c = sums[:, :D] + (sums[:, D : 2 * D] + sums[:, 2 * D :])
            c_ref[rows(b), cols(h)] = c
            last = c[BL - 1 :, :]
            last_ref[pl.ds(h * blocks + b, 1), :] = last
            kt = split(k_ref[rows(b), cols(h)].astype(f32) * jnp.exp(-c))
            qt = split(q_ref[rows(b), cols(h)].astype(f32) * jnp.exp(c))
            kh_ref[rows(b), cols(h)], kl_ref[rows(b), cols(h)] = kt
            qh_ref[rows(b), cols(h)], ql_ref[rows(b), cols(h)] = qt
            kv = tn((value_tilde(b, h, shrink), kt))
            start_ref[h * blocks + b] = state
            return jnp.exp(last - span * down) * (state + kv), key_sum + last

        state, key_sum = lax.fori_loop(
            0, blocks, block, (jnp.zeros((D, D), f32), jnp.zeros((1, D), f32)), unroll=UNROLL
        )
        local_ref[h] = state
        total_ref[pl.ds(h, 1), :] = key_sum
        return 0

    lax.fori_loop(0, heads, prepare, 0)
    pl.semaphore_wait(barrier, n - 1 + n_head - 1)

    def device_decay(h):
        return jnp.exp(total_ref[pl.ds(h, 1), :] - float(rows_all) * rate_down(h))

    def chain(h, first, last, device, recv, send, recv_sem, send_sem):
        copy = pltpu.make_async_remote_copy(
            src_ref=send.at[h],
            dst_ref=recv.at[h],
            send_sem=send_sem.at[h],
            recv_sem=recv_sem.at[h],
            device_id=device,
            device_id_type=MESH,
        )

        @pl.when(p != first)
        def _():
            copy.wait_recv()

        @pl.when(p != last)
        def _():
            send[h] = device_decay(h) * recv[h] + local_ref[h]
            copy.start()

    def drain(h, last, device, recv, send, recv_sem, send_sem):
        copy = pltpu.make_async_remote_copy(
            src_ref=send.at[h],
            dst_ref=recv.at[h],
            send_sem=send_sem.at[h],
            recv_sem=recv_sem.at[h],
            device_id=device,
            device_id_type=MESH,
        )

        @pl.when(p != last)
        def _():
            copy.wait_send()

    def inside(h, _):
        shrink = jnp.exp(steps_in * rate_row(h))

        def block(b, _):
            qt = pieces(qh_ref, ql_ref, b, h)
            kt = pieces(kh_ref, kl_ref, b, h)
            scores = jnp.where(causal, nt((qt, kt)), 0.0)
            sc_ref[rows(b), cols(h)] = scores
            core_ref[rows(b), cols(h)] = nn((split(scores), value_tilde(b, h, shrink)))
            return 0

        lax.fori_loop(0, blocks, block, 0, unroll=UNROLL)
        return 0

    right = seq_device(lax.rem(p + 1, n))
    left = seq_device(lax.rem(p + n - 1, n))

    @pl.when(p == 0)
    def _():
        fr_ref[...] = jnp.zeros_like(fr_ref)

    @pl.when(p == n - 1)
    def _():
        ar_ref[...] = jnp.zeros_like(ar_ref)

    ahead = jnp.minimum(heads, 3 * p)
    lax.fori_loop(0, ahead, inside, 0)

    def forward_chain(h, _):
        chain(h, 0, n - 1, right, fr_ref, fs_ref, fr_sem, fs_sem)
        return 0

    lax.fori_loop(0, heads, forward_chain, 0)
    lax.fori_loop(ahead, heads, inside, 0)

    sq_ref[...] = jnp.zeros_like(sq_ref)
    cr_ref[...] = jnp.zeros_like(cr_ref)

    def finish_core(h, _):
        down = rate_down(h)
        growth = jnp.exp(-steps_in * rate_row(h))
        gain = gain_ref[pl.ds(h, 1), :]

        def block(b, before):
            decay = jnp.exp(before - (b * BL).astype(f32) * down)
            state = start_ref[h * blocks + b] + decay * fr_ref[h]
            start_ref[h * blocks + b] = state
            core = growth * (
                core_ref[rows(b), cols(h)]
                + nt((pieces(qh_ref, ql_ref, b, h), split(state)))
            )
            core_ref[rows(b), cols(h)] = core
            weighted = og_ref[rows(b), cols(h)].astype(f32) * gain
            sq_ref[rows(b), :] += core * core
            cr_ref[rows(b), :] += weighted * core
            return before + last_row(h, b)

        lax.fori_loop(0, blocks, block, jnp.zeros((1, D), f32), unroll=UNROLL)
        return 0

    lax.fori_loop(0, heads, finish_core, 0)

    for b in range(blocks):
        for ref, place in ((sq_ref, b), (cr_ref, blocks + b)):
            across = ref[b * BL : (b + 1) * BL, :].T
            hs_ref[me, pl.ds(place, 1), :] = jnp.sum(across, axis=0, keepdims=True)

    def head_copy(i):
        peer = lax.rem(me + i, n_head)
        return pltpu.make_async_remote_copy(
            src_ref=hs_ref.at[me],
            dst_ref=hs_ref.at[me],
            send_sem=hs_sem.at[i - 1],
            recv_sem=hr_sem.at[i - 1],
            device_id={"head": peer},
            device_id_type=MESH,
        )

    for i in range(1, n_head):
        head_copy(i).start()
    for i in range(1, n_head):
        head_copy(i).wait_recv()
    sums = hs_ref[0]
    for i in range(1, n_head):
        sums = sums + hs_ref[i]
    columns = float(cols_all * n_head)
    inverse = lax.rsqrt(sums[:blocks] / columns + 1e-06)
    slope = inverse * inverse * inverse * sums[blocks:] / columns
    for b in range(blocks):
        for ref, value in ((sq_ref, inverse), (cr_ref, slope)):
            ref[b * BL : (b + 1) * BL, :] = jnp.broadcast_to(value[b : b + 1], (BL, BL)).T

    def start_adjoint(h, _):
        down = rate_down(h)
        growth = jnp.exp(-steps_in * rate_row(h))
        gain = gain_ref[pl.ds(h, 1), :]

        def block(step, carry):
            adjoint, gain_sum = carry
            b = blocks - 1 - step
            grad_out = og_ref[rows(b), cols(h)].astype(f32)
            core = core_ref[rows(b), cols(h)]
            normed = grad_out * sq_ref[rows(b), :]
            gain_sum = gain_sum + jnp.sum(normed * core, axis=0, keepdims=True)
            gt = split((normed * gain - core * cr_ref[rows(b), :]) * growth)
            gh_ref[rows(b), cols(h)], gl_ref[rows(b), cols(h)] = gt
            end_ref[h * blocks + b] = adjoint
            addend = tn((gt, pieces(qh_ref, ql_ref, b, h)))
            return addend + jnp.exp(last_row(h, b) - span * down) * adjoint, gain_sum

        adjoint, gain_sum = lax.fori_loop(
            0, blocks, block, (jnp.zeros((D, D), f32), jnp.zeros((1, D), f32)), unroll=UNROLL
        )
        local_ref[h] = adjoint
        gs_ref[p, pl.ds(h, 1), :] = gain_sum
        return 0

    lax.fori_loop(0, heads, start_adjoint, 0)

    def middle(h, _):
        shrink = jnp.exp(steps_in * rate_row(h))

        def block(b, _):
            gt = pieces(gh_ref, gl_ref, b, h)
            qt = pieces(qh_ref, ql_ref, b, h)
            kt = pieces(kh_ref, kl_ref, b, h)
            mixed = split(jnp.where(causal, nt((gt, value_tilde(b, h, shrink))), 0.0))
            state = split(start_ref[h * blocks + b])
            scores = split(sc_ref[rows(b), cols(h)])
            query_part = jnp.exp(c_ref[rows(b), cols(h)]) * nn((gt, state), (mixed, kt))
            qg_ref[rows(b), cols(h)] = query_part.astype(bf16)
            core_ref[rows(b), cols(h)] = tn((mixed, qt))
            sc_ref[rows(b), cols(h)] = tn((scores, gt))
            return 0

        lax.fori_loop(0, blocks, block, 0, unroll=UNROLL)
        return 0

    def gain_copy(i):
        return pltpu.make_async_remote_copy(
            src_ref=gs_ref.at[p],
            dst_ref=gs_ref.at[p],
            send_sem=gs_sem.at[i - 1],
            recv_sem=gr_sem.at[i - 1],
            device_id=seq_device(lax.rem(p + i, n)),
            device_id_type=MESH,
        )

    ahead = jnp.minimum(heads, n - 1 - p)
    lax.fori_loop(0, ahead, middle, 0)

    def backward_chain(h, _):
        chain(h, n - 1, 0, left, ar_ref, as_ref, ar_sem, as_sem)
        return 0

    lax.fori_loop(0, heads, backward_chain, 0)

    def gain_start(i, _):
        gain_copy(i).start()
        return 0

    lax.fori_loop(1, n, gain_start, 0)
    lax.fori_loop(ahead, heads, middle, 0)

    def finish(h, _):
        down = rate_down(h)
        shrink = jnp.exp(steps_in * rate_row(h))

        def block(step, after):
            b = blocks - 1 - step
            last = last_row(h, b)
            decay = jnp.exp(after - (step * BL).astype(f32) * down)
            end = end_ref[h * blocks + b] + decay * ar_ref[h]
            passed = split(jnp.exp(last - span * down) * end)
            kt = pieces(kh_ref, kl_ref, b, h)
            key_part = jnp.exp(-c_ref[rows(b), cols(h)]) * (
                core_ref[rows(b), cols(h)] + nn((value_tilde(b, h, shrink), passed))
            )
            kg_ref[rows(b), cols(h)] = key_part.astype(bf16)
            value_part = shrink * (sc_ref[rows(b), cols(h)] + nt((kt, passed)))
            vg_ref[rows(b), cols(h)] = value_part.astype(bf16)
            return after + last

        lax.fori_loop(0, blocks, block, jnp.zeros((1, D), f32), unroll=UNROLL)
        return 0

    lax.fori_loop(0, heads, finish, 0)

    def gain_wait(i, _):
        gain_copy(i).wait_recv()
        return 0

    lax.fori_loop(1, n, gain_wait, 0)

    def gain_add(i, total):
        return total + gs_ref[i]

    total = lax.fori_loop(1, n, gain_add, gs_ref[0])
    gg_ref[...] = total / math.sqrt(rows_all * n)

    def drain_all(h, _):
        drain(h, n - 1, right, fr_ref, fs_ref, fr_sem, fs_sem)
        drain(h, 0, left, ar_ref, as_ref, ar_sem, as_sem)
        return 0

    lax.fori_loop(0, heads, drain_all, 0)
    for i in range(1, n_head):
        head_copy(i).wait_send()

    def gain_drain(i, _):
        gain_copy(i).wait_send()
        return 0

    lax.fori_loop(1, n, gain_drain, 0)


UNROLL = 2


def on_device(sizes, queries, keys, values, out_grad, log_key_decay, value_rate, norm_gain):
    t, c = queries.shape
    heads, blocks = c // D, t // BL
    n = sizes[0] * sizes[1]
    n_head = sizes[2]
    vmem = pl.BlockSpec(memory_space=pltpu.VMEM)
    whole = lambda dtype: pltpu.VMEM((t, c), dtype)
    states = lambda count: pltpu.VMEM((count, D, D), f32)
    dma = lambda count: pltpu.SemaphoreType.DMA((count,))
    out = pl.pallas_call(
        functools.partial(kernel, sizes),
        out_shape=[jax.ShapeDtypeStruct((t, c), bf16)] * 3
        + [jax.ShapeDtypeStruct((heads, D), f32)],
        in_specs=[vmem] * 7,
        out_specs=[vmem] * 4,
        scratch_shapes=[
            whole(f32), whole(bf16), whole(bf16), whole(bf16), whole(bf16), whole(bf16),
            whole(bf16), whole(f32), whole(f32), states(heads * blocks), states(heads * blocks),
            pltpu.VMEM((heads * blocks, D), f32), pltpu.VMEM((heads, D), f32), states(heads),
            states(heads), states(heads), states(heads), states(heads),
            pltpu.VMEM((t, D), f32), pltpu.VMEM((t, D), f32),
            pltpu.VMEM((n_head, 2 * blocks, D), f32), pltpu.VMEM((n, heads, D), f32),
            dma(heads), dma(heads), dma(heads), dma(heads),
            dma(max(n_head - 1, 1)), dma(max(n_head - 1, 1)),
            dma(max(n - 1, 1)), dma(max(n - 1, 1)),
        ],
        compiler_params=pltpu.CompilerParams(
            collective_id=0, has_side_effects=True, vmem_limit_bytes=63 * 1024 * 1024
        ),
        name="recurrence_backward",
    )(
        queries,
        keys,
        values,
        out_grad,
        log_key_decay,
        value_rate.reshape(heads, D),
        norm_gain.reshape(heads, D),
    )
    return out[0], out[1], out[2], out[3].reshape(c)


def solution(mesh):
    split_all = P(("outer", "inner"), "head")
    sizes = tuple(mesh.shape[name] for name in ("outer", "inner", "head"))
    return jax.shard_map(
        functools.partial(on_device, sizes),
        mesh=mesh,
        in_specs=(split_all,) * 5 + (P("head"), P("head")),
        out_specs=(split_all,) * 3 + (P("head"),),
        check_vma=False,
    )
```

profile of v0, /device:TPU:0, one launch (start us, length us, event | category | flops | bytes accessed | tf_op | source)
XLA Modules:
  0.0 158.1 jit_solution(3958633574014259284)
XLA Ops:
  0.6 149.9 %recurrence_backward.1 = (bf16[1024,1024]{1,0:T(8,128)(2,1)}, bf16[1024,1024]{1,0:T(8,128)(2,1)}, bf16[1024,1024]{1,0:T(8,128)(2,1)}, f32[8,128]{1,0:T(8,128)}) custom-call(bf16[1024,1024]{1,0:T(8,128)(2,1)} %q_ref.1, bf16[1024,1024]{1,0:T(8,128)(2,1)} %k_ref.1, bf16[1024,1024]{1,0:T(8,128)(2,1)} %v_ref.1, bf16[1024,1024]{1,0:T(8,128)(2,1)} %og_ref.1, ...), custom_call_target="tpu_custom_call" | custom-call | tf_op jit(solution)/shard_map/recurrence_backward/pallas_call | solution.py:412
  150.6 0.0 copy-start.1
  150.6 3.2 %copy.15 = bf16[1024,1024]{1,0:T(8,128)(2,1)} copy(bf16[1024,1024]{1,0:T(8,128)(2,1)} %get-tuple-element.16) | data formatting | bytes 4194304
  153.8 0.0 copy-done.1
  153.8 0.0 copy-start
  153.8 1.3 copy.16
  155.1 1.0 copy-done
  156.2 0.0 copy-start.2
  156.2 1.3 copy.17
  157.5 0.0 copy-done.2
  157.5 0.6 copy.18
Async XLA Ops:
  150.6 3.2 %copy-start.1 = (bf16[1024,1024]{1,0:T(8,128)(2,1)S(1)}, bf16[1024,1024]{1,0:T(8,128)(2,1)}, u32[]{:S(2)}) copy-start(bf16[1024,1024]{1,0:T(8,128)(2,1)} %get-tuple-element.17) | copy-start | bytes 6291460
  153.8 2.3 %copy-start = (bf16[1024,1024]{1,0:T(8,128)(2,1)S(1)}, bf16[1024,1024]{1,0:T(8,128)(2,1)}, u32[]{:S(2)}) copy-start(bf16[1024,1024]{1,0:T(8,128)(2,1)} %get-tuple-element.18) | copy-start | bytes 6291460
  156.2 1.3 copy-start.2
where the time goes:
time: 158 us
  Pallas kernels  150 us (95%)
  local copies, waits for them, and re-layouts  7.5 us (5%)
    pallas_call x1, Pallas kernels, on_device(): pl.pallas_call(functools.partial(kernel, sizes), out_shape=[jax.ShapeDtyp...  150 us
    unnamed x10, local copies, waits for them, and re-layouts  7.5 us

commit v1 on v0

--- a/solution.py
+++ b/solution.py
@@ -28,7 +28,8 @@
 
     total = None
     for (ah, al), (bh, bl) in pairs:
-        part = dot(ah, bh) + (dot(ah, bl) + dot(al, bh))
+        both = dot(ah, jnp.concatenate([bh, bl], axis=1 - right_dim))
+        part = both[:, :D] + (both[:, D:] + dot(al, bh))
         total = part if total is None else total + part
     return total
 
@@ -397,7 +398,7 @@
     lax.fori_loop(1, n, gain_drain, 0)
 
 
-UNROLL = 2
+UNROLL = 4
 
 
 def on_device(sizes, queries, keys, values, out_grad, log_key_decay, value_rate, norm_gain):

time: 158 us -> 140 us (0.89)
  Pallas kernels: 150 us -> 131 us
    pallas_call x1, Pallas kernels: 150 us -> 131 us  [on_device(): pl.pallas_call(functools.partial(kernel, sizes), out_shape=[jax.ShapeDtyp...]
where the time goes in v1:
time: 140 us; the launch traced here: 139 us
  Pallas kernels  131 us (94%)
  local copies, waits for them, and re-layouts  7.5 us (5%)
    pallas_call x1, Pallas kernels, on_device(): pl.pallas_call(functools.partial(kernel, sizes), out_shape=[jax.ShapeDtyp...  131 us
    unnamed x10, local copies, waits for them, and re-layouts  7.5 us

profile of v1, /device:TPU:0, one launch (start us, length us, event | category | flops | bytes accessed | tf_op | source)
XLA Modules:
  0.0 139.3 jit_solution(17783772162320645357)
XLA Ops:
  0.6 131.2 %recurrence_backward.1 = (bf16[1024,1024]{1,0:T(8,128)(2,1)}, bf16[1024,1024]{1,0:T(8,128)(2,1)}, bf16[1024,1024]{1,0:T(8,128)(2,1)}, f32[8,128]{1,0:T(8,128)}) custom-call(bf16[1024,1024]{1,0:T(8,128)(2,1)} %q_ref.1, bf16[1024,1024]{1,0:T(8,128)(2,1)} %k_ref.1, bf16[1024,1024]{1,0:T(8,128)(2,1)} %v_ref.1, bf16[1024,1024]{1,0:T(8,128)(2,1)} %og_ref.1, ...), custom_call_target="tpu_custom_call" | custom-call | tf_op jit(solution)/shard_map/recurrence_backward/pallas_call | solution.py:413
  131.8 0.0 copy-start.1
  131.8 3.2 %copy.15 = bf16[1024,1024]{1,0:T(8,128)(2,1)} copy(bf16[1024,1024]{1,0:T(8,128)(2,1)} %get-tuple-element.16) | data formatting | bytes 4194304
  135.1 0.0 copy-done.1
  135.1 0.0 copy-start
  135.1 1.3 copy.16
  136.4 1.0 copy-done
  137.4 0.0 copy-start.2
  137.4 1.3 copy.17
  138.8 0.0 copy-done.2
  138.8 0.6 copy.18
Async XLA Ops:
  131.8 3.2 %copy-start.1 = (bf16[1024,1024]{1,0:T(8,128)(2,1)S(1)}, bf16[1024,1024]{1,0:T(8,128)(2,1)}, u32[]{:S(2)}) copy-start(bf16[1024,1024]{1,0:T(8,128)(2,1)} %get-tuple-element.17) | copy-start | bytes 6291460
  135.1 2.3 %copy-start = (bf16[1024,1024]{1,0:T(8,128)(2,1)S(1)}, bf16[1024,1024]{1,0:T(8,128)(2,1)}, u32[]{:S(2)}) copy-start(bf16[1024,1024]{1,0:T(8,128)(2,1)} %get-tuple-element.18) | copy-start | bytes 6291460
  137.4 1.3 copy-start.2
